TPU v7x, 128 devices: a whole 4x4x4 slice. The times are simulated.
128 devices in a mesh: occ: 4 (over x), virt: 32 (over y, z, core).
Axes of the slice: x: 4, y: 4, z: 4, core: 2. Of those that a mesh axis runs over, the one named last changes fastest.
Arguments:
- amplitudes: bfloat16 [1, 100, 1024, 1024], P(None, 'occ', 'virt'), may hold values from -6 to 6
- cycle_block: bfloat16 [1024, 100, 4, 1024], P('virt', None, 'occ'), may hold values from -0.01953125 to 0.01953125
- drive_term: bfloat16 [1, 1024, 4, 1024], P(None, 'virt', 'occ'), may hold values from -6 to 6
- occ_energy: float32 [100], replicated, may hold values from -2 to -0.3
- virt_energy: float32 [1024], replicated, may hold values from 0.2 to 4
- occ_irrep: int32 [100], replicated, may hold values from 0 to 1
- virt_irrep: int32 [1024], replicated, may hold values from 0 to 1
- slab_occ: int32 [1], replicated, may hold values from 0 to 99
- col_occ: int32 [4], replicated, may hold values from 0 to 99
Outputs:
- amp_update: float32 [1, 1024, 4, 1024], P(None, 'virt', 'occ')
Inputs may be any that keep to these rules, and one draw needn't show every extreme that they name: `occ_irrep`: labels of the two irreducible representations of the C2 group. `virt_irrep`: labels of the two irreducible representations of the C2 group.
All inputs are finite; a program needn't handle non-finite values.
Results may differ from a plain program's by a relative error of at most 0.0003.
Values may be sent and summed in bfloat16 or wider, within the bound.
A program may use at most 64 MiB of HBM per device.

v0:
```python
import jax
import jax.numpy as jnp
from jax import lax
from jax.sharding import PartitionSpec as P


def pick_entries(values_table, indices):
    hits = indices[:, None] == jnp.arange(values_table.shape[0], dtype=jnp.int32)[None, :]
    return jnp.sum(
        jnp.where(hits, values_table[None, :], jnp.zeros((), values_table.dtype)), axis=1
    )


def body(
    amplitudes,
    cycle_block,
    drive_term,
    occ_energy,
    virt_energy,
    occ_irrep,
    virt_irrep,
    slab_occ,
    col_occ,
):
    k_rows = amplitudes.shape[1]
    a_cols = amplitudes.shape[2]
    j_cols = cycle_block.shape[2]
    occ_pos = lax.axis_index("occ")
    virt_pos = lax.axis_index("virt")
    slab_irrep = pick_entries(occ_irrep, slab_occ)
    col_irrep = pick_entries(occ_irrep, col_occ)
    irr_k = lax.dynamic_slice_in_dim(occ_irrep, occ_pos * k_rows, k_rows)
    irr_a = lax.dynamic_slice_in_dim(virt_irrep, virt_pos * a_cols, a_cols)
    parity = (
        slab_irrep[:, None, None, None]
        + irr_k[None, :, None, None]
        + irr_a[None, None, :, None]
        + virt_irrep[None, None, None, :]
    )
    masked = jnp.where(parity % 2 == 0, amplitudes, jnp.zeros((), amplitudes.dtype))
    pair_block = lax.all_gather(masked, "occ", axis=1, tiled=True)
    relaid = lax.all_to_all(pair_block, "virt", split_axis=3, concat_axis=2, tiled=True)
    partial_value = jnp.einsum(
        "skac,ckjb->sajb", relaid, cycle_block, preferred_element_type=jnp.float32
    )
    cycle_sum = lax.psum_scatter(partial_value, "virt", scatter_dimension=1, tiled=True)
    e_slab = pick_entries(occ_energy, slab_occ)
    e_cols = lax.dynamic_slice_in_dim(pick_entries(occ_energy, col_occ), occ_pos * j_cols, j_cols)
    irr_cols = lax.dynamic_slice_in_dim(col_irrep, occ_pos * j_cols, j_cols)
    e_rows = lax.dynamic_slice_in_dim(virt_energy, virt_pos * a_cols, a_cols)
    divisor = (
        e_rows[None, :, None, None]
        + virt_energy[None, None, None, :]
        - e_slab[:, None, None, None]
        - e_cols[None, None, :, None]
    )
    out_parity = (
        slab_irrep[:, None, None, None]
        + irr_a[None, :, None, None]
        + irr_cols[None, None, :, None]
        + virt_irrep[None, None, None, :]
    )
    value = (drive_term.astype(jnp.float32) + cycle_sum) / divisor
    return jnp.where(out_parity % 2 == 0, value, jnp.zeros((), jnp.float32))


def solution(mesh):
    in_specs = (
        P(None, "occ", "virt", None),
        P("virt", None, "occ", None),
        P(None, "virt", "occ", None),
        P(),
        P(),
        P(),
        P(),
        P(),
        P(),
    )
    out_specs = P(None, "virt", "occ", None)
    return jax.shard_map(body, mesh=mesh, in_specs=in_specs, out_specs=out_specs, check_vma=False)
```

profile of v0, /device:TPU:0, one launch (start us, length us, event | category | flops | bytes accessed | tf_op | source)
XLA Modules:
  0.0 338.4 jit_solution(3754829099605659137)
XLA Ops:
  6.5 0.0 all-gather.2.cloned.1.call-start
  7.2 1.4 fusion.10
  8.6 0.9 select_reduce_fusion.1
  9.4 1.4 dynamic-slice_add_fusion
  10.8 0.6 dynamic_slice.16
  11.4 2.1 add_add_fusion
  13.5 0.1 broadcast_add_fusion
  13.6 3.9 %fusion.4 = bf16[1,25,32,1024]{3,2,0,1:T(8,128)(2,1)} fusion(bf16[1,25,32,1024]{3,2,1,0:T(8,128)(2,1)} %param.9, s32[1024]{0:T(1024)} %param.15, s32[25,32]{1,0:T(8,128)S(1)} %broadcast_add_fusion), kind=kLoop, calls=%fused_computation.9 | loop fusion | flops 11468800 | bytes 3284096 | tf_op jit(solution)/shard_map/jit(_where)/select_n | solution.py:40
  17.4 0.0 all-gather.2.cloned.1.call-update
  17.5 0.0 reduce-scatter.2.cloned.1.call-start
  17.5 70.4 %all-gather.2.cloned.1.call-done = bf16[1,100,32,1024]{3,2,0,1:T(8,128)(2,1)} async-done(((bf16[1,25,32,1024]{3,2,0,1:T(8,128)(2,1)}), bf16[1,100,32,1024]{3,2,0,1:T(8,128)(2,1)}) %all-gather.2.cloned.1.call-update) | async-done | bytes 6553616 | tf_op jit(solution)/shard_map/all_gather | solution.py:41
  87.9 12.9 %copy.25 = bf16[1,100,32,1024]{1,2,0,3:T(8,128)(2,1)} copy(bf16[1,100,32,1024]{3,2,0,1:T(8,128)(2,1)} %all-gather.2.cloned.1.call-done) | data formatting | bytes 13107200 | tf_op jit(solution)/shard_map/all_gather | solution.py:41
  100.8 102.8 %all_to_all.15 = bf16[1,100,32,1024]{1,2,0,3:T(8,128)(2,1)} all-to-all(bf16[1,100,32,1024]{1,2,0,3:T(8,128)(2,1)} %copy.25), channel_id=1, replica_groups=mesh['occ'=4,'virt'=32] {'virt'}, dimensions={3} | all-to-all | bytes 13107200 | tf_op jit(solution)/shard_map/all_to_all | solution.py:42
  203.6 9.8 %copy.26 = bf16[1,100,32,1024]{1,3,2,0:T(8,128)(2,1)} copy(bf16[1,100,32,1024]{1,2,0,3:T(8,128)(2,1)} %all_to_all.15) | data formatting | bytes 13107200 | tf_op jit(solution)/shard_map/all_to_all | solution.py:42
  213.5 9.1 %copy.27 = bf16[1,100,32,32,32]{1,4,3,2,0:T(8,128)(2,1)} copy(bf16[1,100,32,32,32]{1,4,2,3,0:T(8,128)(2,1)} %bitcast.22) | data formatting | bytes 13107200 | tf_op jit(solution)/shard_map/all_to_all | solution.py:42
  222.6 13.4 %copy.28 = bf16[100,1024,32]{1,2,0:T(8,128)(2,1)} copy(bf16[100,1024,32]{0,2,1:T(8,128)(2,1)} %bitcast.21) | data formatting | bytes 13107200 | tf_op jit(solution)/shard_map/reshape.10
  236.0 12.7 %fusion.5 = f32[1,1024,1,1024]{3,1,2,0:T(8,128)} fusion(bf16[100,1024,32]{1,2,0:T(8,128)(2,1)} %copy.28, bf16[32,100,1,1024]{3,0,2,1:T(8,128)(2,1)} %param.10), kind=kOutput, calls=%fused_computation.10 | convolution fusion | flops 6710886400 | bytes 17301504 | tf_op jit(solution)/shard_map/skac,ckjb->sajb/dot_general | solution.py:43
  248.7 0.0 copy-start
  248.7 0.0 copy-start.1
  248.7 0.0 reduce-scatter.2.cloned.1.call-update
  248.7 0.6 copy-done.3
  249.3 0.0 copy-done.4
  249.3 0.2 select_reduce_fusion
  249.5 0.6 dynamic_slice.19
  250.1 0.0 copy-done.2
  250.1 0.1 dynamic_slice.18
  250.2 0.6 fusion.11
  250.8 77.7 %reduce-scatter.2.cloned.1.call-done = f32[1,32,1,1024]{3,1,2,0:T(8,128)} async-done(((f32[1,1024,1,1024]{3,1,2,0:T(8,128)}), f32[1,32,1,1024]{3,1,2,0:T(8,128)}) %reduce-scatter.2.cloned.1.call-update) | async-done | bytes 131088 | tf_op jit(solution)/shard_map/reduce_scatter | solution.py:46
  328.5 0.0 copy-done
  328.5 0.0 copy-done.1
  328.5 2.3 divide_select_fusion
  330.8 0.8 copy.29
  (3 shorter events, 0.0 us)
Async XLA Ops:
  6.5 81.4 %all-gather.2.cloned.1.call-start = ((), (), s32[]{:S(2)}) async-start(), calls=%async_computation.2 | async-start | bytes 8192000 | tf_op jit(solution)/shard_map/all_gather | solution.py:41
  17.5 311.0 %reduce-scatter.2.cloned.1.call-start = ((), (), s32[]{:S(2)}) async-start(), calls=%async_computation.3 | async-start | bytes 4325376 | tf_op jit(solution)/shard_map/reduce_scatter | solution.py:46
  248.7 0.7 copy-start.3
  248.7 0.7 copy-start.4
  248.7 1.4 copy-start.2
  248.7 79.8 %copy-start = (bf16[1,32,1,1024]{3,1,2,0:T(8,128)(2,1)S(1)}, bf16[1,32,1,1024]{3,1,2,0:T(8,128)(2,1)}, u32[]{:S(2)}) copy-start(bf16[1,32,1,1024]{3,1,2,0:T(8,128)(2,1)} %param.11) | copy-start | bytes 196612
  248.7 79.8 %copy-start.1 = (s32[1024]{0:T(1024)S(1)}, s32[1024]{0:T(1024)}, u32[]{:S(2)}) copy-start(s32[1024]{0:T(1024)} %param.15) | copy-start | bytes 12292
Sparse Core Ops, SparseCore 0:
  17.6 70.2 all-gather.1
  248.8 79.5 reduce-scatter.1
where the time goes:
time: 339 us; the launch traced here: 338 us
  waiting for transfers between devices  148 us (44%)
  blocking collectives  103 us (30%)
  local copies, waits for them, and re-layouts  47.9 us (14%)
  between operations  14.1 us (4%)
  other arithmetic  12.8 us (4%)
  matrix products  12.7 us (4%)
    all_to_all x1, blocking collectives, body(): lax.all_to_all(pair_block, 'virt', split_axis=3, concat_axis=2, tiled=True)  103 us
    reduce_scatter x1, waiting for transfers between devices, body(): lax.psum_scatter(partial_value, 'virt', scatter_dimension=1, tiled=True)  77.7 us
    all_gather x1, waiting for transfers between devices, body(): pair_block = lax.all_gather(masked, 'occ', axis=1, tiled=True)  70.4 us
    all_to_all x2, local copies, waits for them, and re-layouts, body(): lax.all_to_all(pair_block, 'virt', split_axis=3, concat_axis=2, tiled=True)  19 us
    another operation x1, local copies, waits for them, and re-layouts  13.4 us
    all_gather x1, local copies, waits for them, and re-layouts, body(): pair_block = lax.all_gather(masked, 'occ', axis=1, tiled=True)  12.9 us
    dot_general x1, matrix products, body(): jnp.einsum('skac,ckjb->sajb', relaid, cycle_block, preferred_element_type...  12.7 us
  transfers between devices with their start and end apart: 2, of which 2 were waited for; matrix products, arithmetic and copies ran while one was open for 0% of the time, Pallas kernels for 0%

commit v1 on v0

--- a/solution.py
+++ b/solution.py
@@ -39,7 +39,12 @@
     )
     masked = jnp.where(parity % 2 == 0, amplitudes, jnp.zeros((), amplitudes.dtype))
     pair_block = lax.all_gather(masked, "occ", axis=1, tiled=True)
-    relaid = lax.all_to_all(pair_block, "virt", split_axis=3, concat_axis=2, tiled=True)
+    relaid = jnp.concatenate(
+        lax.all_to_all(
+            jnp.stack(jnp.split(pair_block, lax.axis_size("virt"), axis=3)), "virt", 0, 0
+        ),
+        axis=2,
+    )
     partial_value = jnp.einsum(
         "skac,ckjb->sajb", relaid, cycle_block, preferred_element_type=jnp.float32
     )

time: 339 us -> 440 us (1.30)
  local copies, waits for them, and re-layouts: 47.9 us -> 147 us
    another operation x1 -> x36, local copies, waits for them, and re-layouts: 13.4 us -> 109 us  [the longest x35 95.3 us: body(): jnp.stack(jnp.split(pair_block, lax.axis_size('virt'), axis=3))]
    unnamed x10 -> x73, local copies, waits for them, and re-layouts: 0.63 us -> 36 us
    all_to_all x2 -> x0, local copies, waits for them, and re-layouts: 19 us -> none  [body(): lax.all_to_all(pair_block, 'virt', split_axis=3, concat_axis=2, tiled=True)]
    all_gather x1 -> x0, local copies, waits for them, and re-layouts: 12.9 us -> none  [body(): pair_block = lax.all_gather(masked, 'occ', axis=1, tiled=True)]
where the time goes in v1:
time: 440 us; the launch traced here: 438 us
  waiting for transfers between devices  149 us (34%)
  local copies, waits for them, and re-layouts  147 us (33%)
  blocking collectives  103 us (23%)
  between operations  14.2 us (3%)
  matrix products  12.8 us (3%)
  other arithmetic  12.7 us (3%)
    all_to_all x1, blocking collectives, body(): lax.all_to_all(jnp.stack(jnp.split(pair_block, lax.axis_size('virt'), axi...  103 us
    another operation x35, local copies, waits for them, and re-layouts, body(): jnp.stack(jnp.split(pair_block, lax.axis_size('virt'), axis=3))  95.3 us
    reduce_scatter x1, waiting for transfers between devices, body(): lax.psum_scatter(partial_value, 'virt', scatter_dimension=1, tiled=True)  78.2 us
    all_gather x1, waiting for transfers between devices, body(): pair_block = lax.all_gather(masked, 'occ', axis=1, tiled=True)  70.4 us
    unnamed x73, local copies, waits for them, and re-layouts  36 us
    another operation x1, local copies, waits for them, and re-layouts  13.4 us
    dot_general x1, matrix products, body(): jnp.einsum('skac,ckjb->sajb', relaid, cycle_block, preferred_element_type...  12.8 us
  transfers between devices with their start and end apart: 2, of which 2 were waited for; matrix products, arithmetic and copies ran while one was open for 0% of the time, Pallas kernels for 0%

profile of v1, /device:TPU:0, one launch (start us, length us, event | category | flops | bytes accessed | tf_op | source)
XLA Modules:
  0.0 437.9 jit_solution(7151434153990848723)
XLA Ops:
  13.4 3.9 fusion.4
  17.4 70.4 %all-gather.2.cloned.1.call-done = bf16[1,100,32,1024]{3,2,0,1:T(8,128)(2,1)} async-done(((bf16[1,25,32,1024]{3,2,0,1:T(8,128)(2,1)}), bf16[1,100,32,1024]{3,2,0,1:T(8,128)(2,1)}) %all-gather.2.cloned.1.call-update) | async-done | bytes 6553616 | tf_op jit(solution)/shard_map/all_gather | solution.py:41
  87.8 7.7 %slice_bitcast_fusion.19 = (bf16[1,1,100,32,32]{4,3,2,1,0:T(8,128)(2,1)}, bf16[1,1,100,32,32]{4,3,2,1,0:T(8,128)(2,1)}, bf16[1,1,100,32,32]{4,3,2,1,0:T(8,128)(2...) fusion(bf16[1,100,32,1024]{3,2,0,1:T(8,128)(2,1)} %all-gather.2, ...), kind=kLoop, calls=%fused_computation.30 | loop fusion | bytes 5324800 | tf_op jit(solution)/shard_map/stack | solution.py:44
  95.4 2.7 copy.65
  98.2 2.7 copy.64
  100.8 2.7 copy.63
  103.5 2.7 copy.62
  106.2 2.7 copy.61
  108.9 2.7 copy.60
  111.6 2.7 copy.59
  114.2 2.7 copy.58
  116.9 2.7 copy.57
  126.2 10.4 %slice_bitcast_fusion = (bf16[1,1,100,32,32]{4,3,2,1,0:T(8,128)(2,1)}, bf16[1,1,100,32,32]{4,3,2,1,0:T(8,128)(2,1)}, bf16[1,1,100,32,32]{4,3,2,1,0:T(8,128)(2,1)...) fusion(bf16[1,100,32,1024]{3,2,0,1:T(8,128)(2,1)} %all-gather.2, ...), kind=kLoop, calls=%fused_computation.11 | loop fusion | bytes 7782400 | tf_op jit(solution)/shard_map/stack | solution.py:44
  138.6 2.7 copy.83
  141.3 2.7 copy.82
  144.0 2.7 copy.81
  146.7 2.7 copy.80
  149.4 2.7 copy.79
  152.1 2.7 copy.78
  154.8 2.7 copy.77
  157.5 2.7 copy.76
  160.2 2.7 copy.75
  162.8 2.7 copy.74
  165.6 2.7 copy.73
  168.2 2.7 copy.72
  170.9 2.7 copy.71
  173.6 2.7 copy.70
  219.1 102.8 %all_to_all.5 = bf16[32,1,100,32,32]{2,4,3,1,0:T(8,128)(2,1)} all-to-all(bf16[32,1,100,32,32]{2,4,3,1,0:T(8,128)(2,1)} %constant_dynamic-update-slice_fusion), channel_id=1, replica_groups=mesh['occ'=4,'virt'=32] {'virt'}, dimensions={0} | all-to-all | bytes 13107200 | tf_op jit(solution)/shard_map/all_to_all | solution.py:43
  321.9 13.4 %copy.85 = bf16[100,1024,32]{1,2,0:T(8,128)(2,1)} copy(bf16[100,1024,32]{0,2,1:T(8,128)(2,1)} %bitcast.84) | data formatting | bytes 13107200 | tf_op jit(solution)/shard_map/reshape.12
  335.3 12.8 %fusion.5 = f32[1,1024,1,1024]{3,1,2,0:T(8,128)} fusion(bf16[100,1024,32]{1,2,0:T(8,128)(2,1)} %copy.85, bf16[32,100,1,1024]{3,0,2,1:T(8,128)(2,1)} %param.10), kind=kOutput, calls=%fused_computation.10 | convolution fusion | flops 6710886400 | bytes 17301504 | tf_op jit(solution)/shard_map/skac,ckjb->sajb/dot_general | solution.py:48
  349.7 78.2 %reduce-scatter.2.cloned.1.call-done = f32[1,32,1,1024]{3,1,2,0:T(8,128)} async-done(((f32[1,1024,1,1024]{3,1,2,0:T(8,128)}), f32[1,32,1,1024]{3,1,2,0:T(8,128)}) %reduce-scatter.2.cloned.1.call-update) | async-done | bytes 131088 | tf_op jit(solution)/shard_map/reduce_scatter | solution.py:51
  427.9 2.3 divide_select_fusion
  (98 shorter events, 60.0 us)
Async XLA Ops:
  6.5 81.3 %all-gather.2.cloned.1.call-start = ((), (), s32[]{:S(2)}) async-start(), calls=%async_computation.2 | async-start | bytes 8192000 | tf_op jit(solution)/shard_map/all_gather | solution.py:41
  17.3 410.6 %reduce-scatter.2.cloned.1.call-start = ((), (), s32[]{:S(2)}) async-start(), calls=%async_computation.3 | async-start | bytes 4325376 | tf_op jit(solution)/shard_map/reduce_scatter | solution.py:51
  178.1 21.9 %copy-start.3 = (bf16[1,1,100,32,32]{2,4,3,1,0:T(8,128)(2,1)S(1)}, bf16[1,1,100,32,32]{2,4,3,1,0:T(8,128)(2,1)}, u32[]{:S(2)}) copy-start(bf16[1,1,100,32,32]{2,4,3,1,0:T(8,128)(2,1)} %copy.64) | copy-start | bytes 614404
  178.2 22.6 %copy-start.1 = (bf16[1,1,100,32,32]{2,4,3,1,0:T(8,128)(2,1)S(1)}, bf16[1,1,100,32,32]{2,4,3,1,0:T(8,128)(2,1)}, u32[]{:S(2)}) copy-start(bf16[1,1,100,32,32]{2,4,3,1,0:T(8,128)(2,1)} %copy.65) | copy-start | bytes 614404
  179.8 35.0 %copy-start.6 = (bf16[1,1,100,32,32]{2,4,3,1,0:T(8,128)(2,1)S(1)}, bf16[1,1,100,32,32]{2,4,3,1,0:T(8,128)(2,1)}, u32[]{:S(2)}) copy-start(bf16[1,1,100,32,32]{2,4,3,1,0:T(8,128)(2,1)} %copy.79) | copy-start | bytes 614404
  179.8 35.7 %copy-start.5 = (bf16[1,1,100,32,32]{2,4,3,1,0:T(8,128)(2,1)S(1)}, bf16[1,1,100,32,32]{2,4,3,1,0:T(8,128)(2,1)}, u32[]{:S(2)}) copy-start(bf16[1,1,100,32,32]{2,4,3,1,0:T(8,128)(2,1)} %copy.80) | copy-start | bytes 614404
  179.8 36.4 %copy-start.4 = (bf16[1,1,100,32,32]{2,4,3,1,0:T(8,128)(2,1)S(1)}, bf16[1,1,100,32,32]{2,4,3,1,0:T(8,128)(2,1)}, u32[]{:S(2)}) copy-start(bf16[1,1,100,32,32]{2,4,3,1,0:T(8,128)(2,1)} %copy.81) | copy-start | bytes 614404
  179.8 37.1 %copy-start.2 = (bf16[1,1,100,32,32]{2,4,3,1,0:T(8,128)(2,1)S(1)}, bf16[1,1,100,32,32]{2,4,3,1,0:T(8,128)(2,1)}, u32[]{:S(2)}) copy-start(bf16[1,1,100,32,32]{2,4,3,1,0:T(8,128)(2,1)} %copy.82) | copy-start | bytes 614404
  181.5 31.9 %copy-start.8 = (bf16[1,1,100,32,32]{2,4,3,1,0:T(8,128)(2,1)S(1)}, bf16[1,1,100,32,32]{2,4,3,1,0:T(8,128)(2,1)}, u32[]{:S(2)}) copy-start(bf16[1,1,100,32,32]{2,4,3,1,0:T(8,128)(2,1)} %copy.77) | copy-start | bytes 614404
  181.5 32.6 %copy-start.7 = (bf16[1,1,100,32,32]{2,4,3,1,0:T(8,128)(2,1)S(1)}, bf16[1,1,100,32,32]{2,4,3,1,0:T(8,128)(2,1)}, u32[]{:S(2)}) copy-start(bf16[1,1,100,32,32]{2,4,3,1,0:T(8,128)(2,1)} %copy.78) | copy-start | bytes 614404
  181.5 36.2 %copy-start = (bf16[1,1,100,32,32]{2,4,3,1,0:T(8,128)(2,1)S(1)}, bf16[1,1,100,32,32]{2,4,3,1,0:T(8,128)(2,1)}, u32[]{:S(2)}) copy-start(bf16[1,1,100,32,32]{2,4,3,1,0:T(8,128)(2,1)} %copy.83) | copy-start | bytes 614404
  183.1 25.1 %copy-start.15 = (bf16[1,1,100,32,32]{2,4,3,1,0:T(8,128)(2,1)S(1)}, bf16[1,1,100,32,32]{2,4,3,1,0:T(8,128)(2,1)}, u32[]{:S(2)}) copy-start(bf16[1,1,100,32,32]{2,4,3,1,0:T(8,128)(2,1)} %copy.70) | copy-start | bytes 614404
  183.1 25.8 %copy-start.14 = (bf16[1,1,100,32,32]{2,4,3,1,0:T(8,128)(2,1)S(1)}, bf16[1,1,100,32,32]{2,4,3,1,0:T(8,128)(2,1)}, u32[]{:S(2)}) copy-start(bf16[1,1,100,32,32]{2,4,3,1,0:T(8,128)(2,1)} %copy.71) | copy-start | bytes 614404
  183.1 26.5 %copy-start.13 = (bf16[1,1,100,32,32]{2,4,3,1,0:T(8,128)(2,1)S(1)}, bf16[1,1,100,32,32]{2,4,3,1,0:T(8,128)(2,1)}, u32[]{:S(2)}) copy-start(bf16[1,1,100,32,32]{2,4,3,1,0:T(8,128)(2,1)} %copy.72) | copy-start | bytes 614404
  183.1 27.3 %copy-start.12 = (bf16[1,1,100,32,32]{2,4,3,1,0:T(8,128)(2,1)S(1)}, bf16[1,1,100,32,32]{2,4,3,1,0:T(8,128)(2,1)}, u32[]{:S(2)}) copy-start(bf16[1,1,100,32,32]{2,4,3,1,0:T(8,128)(2,1)} %copy.73) | copy-start | bytes 614404
  183.1 28.0 %copy-start.11 = (bf16[1,1,100,32,32]{2,4,3,1,0:T(8,128)(2,1)S(1)}, bf16[1,1,100,32,32]{2,4,3,1,0:T(8,128)(2,1)}, u32[]{:S(2)}) copy-start(bf16[1,1,100,32,32]{2,4,3,1,0:T(8,128)(2,1)} %copy.74) | copy-start | bytes 614404
  183.1 28.7 %copy-start.10 = (bf16[1,1,100,32,32]{2,4,3,1,0:T(8,128)(2,1)S(1)}, bf16[1,1,100,32,32]{2,4,3,1,0:T(8,128)(2,1)}, u32[]{:S(2)}) copy-start(bf16[1,1,100,32,32]{2,4,3,1,0:T(8,128)(2,1)} %copy.75) | copy-start | bytes 614404
  183.1 29.4 %copy-start.9 = (bf16[1,1,100,32,32]{2,4,3,1,0:T(8,128)(2,1)S(1)}, bf16[1,1,100,32,32]{2,4,3,1,0:T(8,128)(2,1)}, u32[]{:S(2)}) copy-start(bf16[1,1,100,32,32]{2,4,3,1,0:T(8,128)(2,1)} %copy.76) | copy-start | bytes 614404
  335.3 12.8 %copy-start.19 = (s32[4]{0:T(128)S(1)}, s32[4]{0:T(128)}, u32[]{:S(2)}) copy-start(s32[4]{0:T(128)} %param.17) | copy-start | bytes 52
  335.3 12.9 %copy-start.20 = (f32[100]{0:T(128)S(1)}, f32[100]{0:T(128)}, u32[]{:S(2)}) copy-start(f32[100]{0:T(128)} %param.12) | copy-start | bytes 1204
  335.3 13.6 %copy-start.18 = (f32[1024]{0:T(1024)S(1)}, f32[1024]{0:T(1024)}, u32[]{:S(2)}) copy-start(f32[1024]{0:T(1024)} %param.13) | copy-start | bytes 12292
  335.3 92.6 %copy-start.16 = (bf16[1,32,1,1024]{3,1,2,0:T(8,128)(2,1)S(1)}, bf16[1,32,1,1024]{3,1,2,0:T(8,128)(2,1)}, u32[]{:S(2)}) copy-start(bf16[1,32,1,1024]{3,1,2,0:T(8,128)(2,1)} %param.11) | copy-start | bytes 196612
  335.3 92.6 %copy-start.17 = (s32[1024]{0:T(1024)S(1)}, s32[1024]{0:T(1024)}, u32[]{:S(2)}) copy-start(s32[1024]{0:T(1024)} %param.15) | copy-start | bytes 12292
Sparse Core Ops, SparseCore 0:
  17.4 70.2 all-gather.1
  348.3 79.5 reduce-scatter.1
